TPU v7x, 32 devices: a whole 2x2x4 slice. The times are simulated.
32 devices in a mesh: clips: 2 (over x), rows: 16 (over z, y, core).
Axes of the slice: x: 2, y: 2, z: 4, core: 2. Of those that a mesh axis runs over, the one named last changes fastest.
Arguments:
- latents: bfloat16 [8, 64, 160, 384], P('clips', 'rows'), parts along dimension 0, may hold values from -6 to 6
- gamma: float32 [384], replicated, may hold values from 0.5 to 1.5
- weight: bfloat16 [3, 3, 3, 384, 384], replicated, may hold values from -0.0625 to 0.0625
- bias: float32 [384], replicated, may hold values from -3 to 3
- intersection: int32 [32], P('clips'), parts along dimension 0, may hold values from 0 to 2
- ramp: int32 [32], P('clips'), parts along dimension 0, may hold values from 1 to 3
Outputs:
- decoded: bfloat16 [8, 64, 160, 384], P('clips', 'rows'), parts along dimension 0
There are 2 independent parts, one for each index of `clips`. A program takes and returns all parts, laid end to end along the dimension named above; an argument that names none is the same for every part. Nothing has to cross between parts.
All inputs are finite; a program needn't handle non-finite values.
Results may differ from a plain program's by a relative error of at most 0.0034.
Values may be sent and summed in bfloat16 or wider, within the bound.
A program may use at most 448 MiB of HBM per device.

v0:
```python
import functools

import jax
import jax.numpy as jnp
from jax import lax
from jax.experimental import pallas as pl
from jax.experimental.pallas import tpu as pltpu
from jax.sharding import PartitionSpec as P

TAPS = 3
MESH = pl.DeviceIdType.MESH

ROW_OF = ((1, 2), (0, 3))


def kernel(
    frames, width, chans, count,
    x_ref, w_ref, gamma_ref, bias_ref, inter_hbm, ramp_hbm,
    out_ref,
    xbuf, top, bot, lhs, wbuf, acc, ost, inter_ref, ramp_ref,
    xsem, wsem, osem, ssem, send_sem, recv_sem,
):
    me = lax.axis_index("rows")
    span = TAPS * chans
    last = xbuf.shape[1] - 1

    def x_copy(f):
        return pltpu.make_async_copy(x_ref.at[f], xbuf.at[f], xsem.at[f])

    def w_copy(t):
        return pltpu.make_async_copy(
            w_ref.at[TAPS - 1 - t], wbuf.at[:, pl.ds(t * chans, chans)], wsem.at[t]
        )

    down = pltpu.make_async_remote_copy(
        src_ref=x_ref.at[:, last], dst_ref=top, send_sem=send_sem.at[0],
        recv_sem=recv_sem.at[0], device_id={"rows": me + 1}, device_id_type=MESH,
    )
    up = pltpu.make_async_remote_copy(
        src_ref=x_ref.at[:, 0], dst_ref=bot, send_sem=send_sem.at[1],
        recv_sem=recv_sem.at[1], device_id={"rows": me - 1}, device_id_type=MESH,
    )

    small = (
        pltpu.make_async_copy(inter_hbm, inter_ref, ssem.at[0]),
        pltpu.make_async_copy(ramp_hbm, ramp_ref, ssem.at[1]),
    )
    for copy in small:
        copy.start()
    for f in range(frames):
        x_copy(f).start()
    for t in range(TAPS):
        w_copy(t).start()

    barrier = pltpu.get_barrier_semaphore()

    @pl.when(me > 0)
    def _():
        pl.semaphore_signal(
            barrier, inc=1, device_id={"rows": me - 1}, device_id_type=MESH
        )

    @pl.when(me < count - 1)
    def _():
        pl.semaphore_signal(
            barrier, inc=1, device_id={"rows": me + 1}, device_id_type=MESH
        )

    peers = jnp.where(me > 0, 1, 0) + jnp.where(me < count - 1, 1, 0)
    pl.semaphore_wait(barrier, peers)

    @pl.when(me < count - 1)
    def _():
        down.start()

    @pl.when(me > 0)
    def _():
        up.start()

    for copy in small:
        copy.wait()

    before = jnp.maximum(me - 1, 0)
    prev_ov = jnp.where(me > 0, inter_ref[before], 0)
    own_ov = jnp.where(me == count - 1, 0, inter_ref[me])
    ovv = jnp.full((1, chans), prev_ov, jnp.int32)
    ownv = jnp.full((1, chans), own_ov, jnp.int32)
    rampv = jnp.full((1, chans), ramp_ref[before], jnp.int32).astype(jnp.float32)
    a0 = jnp.where(ovv > 0, jnp.maximum(rampv, 0.0) / (rampv + 1.0), 0.0)
    a1 = jnp.where(ovv > 1, jnp.maximum(rampv - 1.0, 0.0) / (rampv + 1.0), 0.0)
    s1 = jnp.where(ovv > 1, 1.0, 1.0 - a0)
    s2 = 1.0 - a1
    live = jnp.where(ownv > 0, 1.0, 0.0)
    gamma = gamma_ref[...].reshape(1, chans)
    bias = bias_ref[...].reshape(1, chans)
    columns = lax.broadcasted_iota(jnp.int32, (width, chans), 0)

    def activate(values):
        square = jnp.mean(values * values, axis=-1, keepdims=True)
        half = values * lax.rsqrt(square + 1e-06) * (0.5 * gamma)
        return half + half * jnp.tanh(half)

    def place(f, value, targets):
        left = jnp.where(columns == 0, 0.0, pltpu.roll(value, 1, 0))
        right = jnp.where(columns == width - 1, 0.0, pltpu.roll(value, width - 1, 0))
        for scale, spots in targets:
            for step_w, part in enumerate((left, value, right)):
                if scale is not None:
                    part = part * scale
                part = part.astype(jnp.bfloat16)
                for half, slot, step_h in spots:
                    lhs[
                        half, f, slot * width : (slot + 1) * width,
                        step_h * span + step_w * chans : step_h * span + (step_w + 1) * chans,
                    ] = part

    own_targets = (
        ((None, ((1, 0, 1), (0, 0, 0))),),
        ((None, ((0, 0, 1), (0, 1, 0))), (s1, ((1, 0, 2),))),
        ((None, ((0, 1, 1), (1, 1, 0))), (s2, ((0, 0, 2),))),
        ((None, ((0, 1, 2), (1, 1, 1))),),
    )

    def own_frame(f, carry):
        x_copy(f).wait()
        for row in range(last + 1):
            values = xbuf[f, row].astype(jnp.float32)
            place(f, activate(values), own_targets[row])
        return carry

    lax.fori_loop(0, frames, own_frame, 0)

    written = set()

    def multiply(half, start, stop, t0, t1):
        block = lhs[half, start:stop].reshape((stop - start) * 2 * width, TAPS * span)
        product = jnp.dot(
            block, wbuf[:, t0 * chans : t1 * chans], preferred_element_type=jnp.float32
        )
        for f in range(start, stop):
            for t in range(t0, t1):
                part = product[
                    (f - start) * 2 * width : (f - start + 1) * 2 * width,
                    (t - t0) * chans : (t - t0 + 1) * chans,
                ]
                if (half, f + t) in written:
                    acc[half, f + t] += part
                else:
                    acc[half, f + t] = part
                    written.add((half, f + t))

    def out_copy(half, f, slot):
        row = ROW_OF[half][slot]
        return pltpu.make_async_copy(
            ost.at[f, row], out_ref.at[f, row], osem.at[f, row]
        )

    def finish(half, start, stop):
        for f in range(start, stop):
            for slot in range(2):
                row = ROW_OF[half][slot]
                total = acc[half, f, slot * width : (slot + 1) * width]
                total = total + (xbuf[f, row].astype(jnp.float32) + bias)
                ost[f, row] = total.astype(jnp.bfloat16)
                out_copy(half, f, slot).start()

    def work(half):
        multiply(half, 0, frames - 1, 0, 2)
        finish(half, 0, frames - 2)
        multiply(half, 0, frames - 2, 2, 3)
        finish(half, frames - 2, frames - 1)
        multiply(half, frames - 1, frames, 0, 1)
        finish(half, frames - 1, frames)

    for t in range(TAPS):
        w_copy(t).wait()
    work(0)

    @pl.when(me > 0)
    def _():
        down.wait_recv()

    @pl.when(me == 0)
    def _():
        top[...] = jnp.zeros(top.shape, top.dtype)

    @pl.when(me < count - 1)
    def _():
        up.wait_recv()

    @pl.when(me == count - 1)
    def _():
        bot[...] = jnp.zeros(bot.shape, bot.dtype)

    def edge_frame(f, carry):
        place(f, activate(top[f].astype(jnp.float32)), ((a0, ((1, 0, 0),)),))
        place(f, activate(bot[f].astype(jnp.float32)), ((live, ((1, 1, 2),)),))
        return carry

    lax.fori_loop(0, frames, edge_frame, 0)
    work(1)

    for half in range(2):
        for f in range(frames):
            for slot in range(2):
                out_copy(half, f, slot).wait()

    @pl.when(me < count - 1)
    def _():
        down.wait_send()

    @pl.when(me > 0)
    def _():
        up.wait_send()


def hand_on(frames, rows, from_ref, to_ref, held, in_sem, out_sem):
    blocks = [(f, r) for f in range(frames) for r in range(rows)]
    fetch = [
        pltpu.make_async_copy(from_ref.at[at], held.at[at], in_sem.at[at])
        for at in blocks
    ]
    store = [
        pltpu.make_async_copy(held.at[at], to_ref.at[at], out_sem.at[at])
        for at in blocks
    ]
    for copy in fetch:
        copy.start()
    for arriving, leaving in zip(fetch, store):
        arriving.wait()
        leaving.start()
    for copy in store:
        copy.wait()


def per_device(latents, gamma, weight, bias, intersection, ramp):
    frames, rows, width, chans = latents.shape
    count = lax.axis_size("rows")
    taps = weight.reshape(TAPS, TAPS * TAPS * chans, chans)
    depth = taps.shape[1]
    hbm = pl.BlockSpec(memory_space=pltpu.HBM)
    vmem = pl.BlockSpec(memory_space=pltpu.VMEM)
    made = pl.pallas_call(
        functools.partial(kernel, frames, width, chans, count),
        out_shape=jax.ShapeDtypeStruct(latents.shape, latents.dtype),
        in_specs=[hbm, hbm, vmem, vmem, hbm, hbm],
        out_specs=hbm,
        scratch_shapes=[
            pltpu.VMEM((frames, rows, width, chans), jnp.bfloat16),
            pltpu.VMEM((frames, width, chans), jnp.bfloat16),
            pltpu.VMEM((frames, width, chans), jnp.bfloat16),
            pltpu.VMEM((2, frames, 2 * width, depth), jnp.bfloat16),
            pltpu.VMEM((depth, TAPS * chans), jnp.bfloat16),
            pltpu.VMEM((2, frames, 2 * width, chans), jnp.float32),
            pltpu.VMEM((frames, rows, width, chans), jnp.bfloat16),
            pltpu.SMEM(intersection.shape, jnp.int32),
            pltpu.SMEM(ramp.shape, jnp.int32),
            pltpu.SemaphoreType.DMA((frames,)),
            pltpu.SemaphoreType.DMA((TAPS,)),
            pltpu.SemaphoreType.DMA((frames, rows)),
            pltpu.SemaphoreType.DMA((2,)),
            pltpu.SemaphoreType.DMA((2,)),
            pltpu.SemaphoreType.DMA((2,)),
        ],
        compiler_params=pltpu.CompilerParams(
            collective_id=0, has_side_effects=True, vmem_limit_bytes=64 * 1024 * 1024
        ),
    )(latents, taps, gamma, bias, intersection, ramp)
    return pl.pallas_call(
        functools.partial(hand_on, frames, rows),
        out_shape=jax.ShapeDtypeStruct(latents.shape, latents.dtype),
        in_specs=[hbm],
        out_specs=hbm,
        scratch_shapes=[
            pltpu.VMEM((frames, rows, width, chans), jnp.bfloat16),
            pltpu.SemaphoreType.DMA((frames, rows)),
            pltpu.SemaphoreType.DMA((frames, rows)),
        ],
        compiler_params=pltpu.CompilerParams(vmem_limit_bytes=64 * 1024 * 1024),
    )(made)


def solution(mesh):
    in_specs = (P("clips", "rows", None, None), P(), P(), P(), P("clips"), P("clips"))
    out_specs = P("clips", "rows", None, None)
    return jax.shard_map(
        per_device, mesh=mesh, in_specs=in_specs, out_specs=out_specs, check_vma=False
    )
```

profile of v0, /device:TPU:1, one launch (start us, length us, event | category | flops | bytes accessed | tf_op | source)
XLA Modules:
  0.0 30.2 jit_solution(7899431851345634215)
XLA Ops:
  0.0 27.5 %shard_map.64.from_ref = bf16[4,4,160,384]{3,2,1,0:T(8,128)(2,1)} custom-call(bf16[4,4,160,384]{3,2,1,0:T(8,128)(2,1)} %x_ref.1, bf16[3,3456,384]{2,1,0:T(8,128)(2,1)} %bitcast.1, f32[384]{0:T(512)} %gamma_ref.1, f32[384]{0:T(512)} %bias_ref.1, s32[16]{0:T(128)} %inter_hbm.1, s32[16]{0:T(128)} %ramp_hbm.1), custom_call_target="tpu_custom_call" | custom-call | tf_op jit(solution)/shard_map/pallas_call | solution.py:243
  27.5 2.5 %shard_map.65 = bf16[4,4,160,384]{3,2,1,0:T(8,128)(2,1)} custom-call(bf16[4,4,160,384]{3,2,1,0:T(8,128)(2,1)} %shard_map.64.from_ref), custom_call_target="tpu_custom_call" | custom-call | tf_op jit(solution)/shard_map/pallas_call | solution.py:269
where the time goes:
time: 30.4 us; the launch traced here: 30.2 us
  Pallas kernels  30.1 us (99%)
    pallas_call x1, Pallas kernels, per_device(): pl.pallas_call(functools.partial(kernel, frames, width, chans, count), ou...  27.5 us
    pallas_call x1, Pallas kernels, per_device(): pl.pallas_call(functools.partial(hand_on, frames, rows), out_shape=jax.Sh...  2.53 us

commit v1 on v0

v1 whole, which is shorter than its diff:
```python
import functools

import jax
import jax.numpy as jnp
from jax import lax
from jax.experimental import pallas as pl
from jax.experimental.pallas import tpu as pltpu
from jax.sharding import PartitionSpec as P

TAPS = 3
POINTS = 4
MESH = pl.DeviceIdType.MESH
PAD = 8
LANES = 128
RING = 8

ABOVE, ROW0, ROW1, ROW1S, ROW2, ROW2S, ROW3, BELOW = range(8)
ROW_OF = ((1, 2), (0, 3))
READS = (
    ((ROW0, ROW1, ROW2S), (ROW1, ROW2, ROW3)),
    ((ABOVE, ROW0, ROW1S), (ROW2, ROW3, BELOW)),
)
UNITS = (
    ((0,), (0, 1), ((0, 1),)),
    ((0,), (2,), ((2,),)),
    ((1,), (1,), ((0,),)),
    ((2, 1), (2, 3), ((0, 1), (1, 2))),
    ((3,), (3,), ((0,),)),
)


def kernel(
    frames, width, chans, count,
    x_ref, w_ref, gamma_ref, bias_ref, inter_hbm, ramp_hbm,
    out_ref,
    xbuf, top, bot, wbuf, gbuf, dbuf, act, ybuf, obuf, inter_ref, ramp_ref,
    xsem, wsem, ssem, send_sem, recv_sem,
):
    me = lax.axis_index("rows")
    last = xbuf.shape[1] - 1
    half_w = width // 2

    def x_copy(f):
        return pltpu.make_async_copy(x_ref.at[f], xbuf.at[f], xsem.at[f])

    def w_copy(t, k):
        return pltpu.make_async_copy(
            w_ref.at[TAPS - 1 - t, :, k], wbuf.at[t, :, k], wsem.at[t, k]
        )

    def down(f):
        return pltpu.make_async_remote_copy(
            src_ref=x_ref.at[f, last], dst_ref=top.at[f], send_sem=send_sem.at[0, f],
            recv_sem=recv_sem.at[0, f], device_id={"rows": me + 1}, device_id_type=MESH,
        )

    def up(f):
        return pltpu.make_async_remote_copy(
            src_ref=x_ref.at[f, 0], dst_ref=bot.at[f], send_sem=send_sem.at[1, f],
            recv_sem=recv_sem.at[1, f], device_id={"rows": me - 1}, device_id_type=MESH,
        )

    small = (
        pltpu.make_async_copy(inter_hbm, inter_ref, ssem.at[0]),
        pltpu.make_async_copy(ramp_hbm, ramp_ref, ssem.at[1]),
    )
    barrier = pltpu.get_barrier_semaphore()

    @pl.when(me > 0)
    def _():
        pl.semaphore_signal(
            barrier, inc=1, device_id={"rows": me - 1}, device_id_type=MESH
        )

    @pl.when(me < count - 1)
    def _():
        pl.semaphore_signal(
            barrier, inc=1, device_id={"rows": me + 1}, device_id_type=MESH
        )

    for copy in small:
        copy.start()
    for f in range(frames):
        x_copy(f).start()
    for t, k in ((0, 0), (1, 0), (0, 2), (1, 2), (2, 0), (2, 2), (0, 1), (1, 1), (2, 1)):
        w_copy(t, k).start()

    @pl.when(me == 0)
    def _():
        top[...] = jnp.zeros(top.shape, top.dtype)

    @pl.when(me == count - 1)
    def _():
        bot[...] = jnp.zeros(bot.shape, bot.dtype)

    for b in range(RING):
        for c in range(chans // LANES):
            act[b, c, 0:PAD] = jnp.zeros((PAD, LANES), jnp.float32)
            act[b, c, PAD + width : PAD + width + PAD] = jnp.zeros(
                (PAD, LANES), jnp.float32
            )

    peers = jnp.where(me > 0, 1, 0) + jnp.where(me < count - 1, 1, 0)
    pl.semaphore_wait(barrier, peers)

    @pl.when(me < count - 1)
    def _():
        for f in range(frames):
            down(f).start()

    @pl.when(me > 0)
    def _():
        for f in range(frames):
            up(f).start()

    for copy in small:
        copy.wait()

    before = jnp.maximum(me - 1, 0)
    prev_ov = jnp.where(me > 0, inter_ref[before], 0)
    own_ov = jnp.where(me == count - 1, 0, inter_ref[me])
    ovv = jnp.full((1, chans), prev_ov, jnp.int32)
    ownv = jnp.full((1, chans), own_ov, jnp.int32)
    rampv = jnp.full((1, chans), ramp_ref[before], jnp.int32).astype(jnp.float32)
    a0 = jnp.where(ovv > 0, jnp.maximum(rampv, 0.0) / (rampv + 1.0), 0.0)
    a1 = jnp.where(ovv > 1, jnp.maximum(rampv - 1.0, 0.0) / (rampv + 1.0), 0.0)
    s1 = jnp.where(ovv > 1, 1.0, 1.0 - a0)
    s2 = 1.0 - a1
    live = jnp.where(ownv > 0, 1.0, 0.0)
    half_gamma = 0.5 * gamma_ref[...].reshape(1, chans)
    bias = bias_ref[...].reshape(1, chans)
    ring = [0]

    def activate(f, source, targets):
        values = source.astype(jnp.float32)
        square = jnp.mean(values * values, axis=-1, keepdims=True)
        half = values * lax.rsqrt(square + 1e-06) * half_gamma
        b = ring[0] % RING
        ring[0] += 1
        value = half + half * jnp.tanh(half)
        for c in range(chans // LANES):
            lanes = slice(c * LANES, (c + 1) * LANES)
            act[b, c, PAD : PAD + width] = value[:, lanes]
            parts = [
                act[b, c, pl.ds(PAD + at, half_w, stride=2)] for at in (-1, 0, 1, 2)
            ]
            for version, scale in targets:
                odd_b, even, odd, even_a = [
                    (part if scale is None else part * scale[:, lanes]).astype(
                        jnp.bfloat16
                    )
                    for part in parts
                ]
                dbuf[0, f, version, :, lanes] = odd_b - odd
                dbuf[1, f, version, :, lanes] = even + odd
                dbuf[2, f, version, :, lanes] = odd - even
                dbuf[3, f, version, :, lanes] = even - even_a

    own_targets = (
        ((ROW0, None),),
        ((ROW1, None), (ROW1S, s1)),
        ((ROW2, None), (ROW2S, s2)),
        ((ROW3, None),),
    )

    def own(f, row):
        activate(f, xbuf[f, row], own_targets[row])

    def edge(f):
        activate(f, top[f], ((ABOVE, a0),))
        activate(f, bot[f], ((BELOW, live),))

    def add_weights(t, h):
        g0, g1, g2 = [wbuf[t, h, k].astype(jnp.float32) for k in range(TAPS)]
        both = g0 + g2
        gbuf[0, t, h] = (both + g1).astype(jnp.bfloat16)
        gbuf[1, t, h] = (both - g1).astype(jnp.bfloat16)

    def filters(p, t):
        if p in (0, 3):
            k = 0 if p == 0 else TAPS - 1
            return jnp.concatenate([wbuf[t, h, k] for h in range(TAPS)], axis=0)
        return jnp.concatenate([gbuf[p - 1, t, h] for h in range(TAPS)], axis=0)

    written = set()

    def multiply(half, unit, p):
        sources, outputs, taps = UNITS[unit]
        left = jnp.concatenate(
            [
                jnp.concatenate(
                    [dbuf[p, f, version] for f in sources for version in reads], axis=1
                )
                for reads in READS[half]
            ],
            axis=0,
        )
        right = jnp.concatenate(
            [
                jnp.concatenate([filters(p, t) for t in across], axis=1)
                if len(across) > 1 else filters(p, across[0])
                for across in taps
            ],
            axis=0,
        )
        product = jnp.dot(left, right, preferred_element_type=jnp.float32)
        for n, o in enumerate(outputs):
            part = product[:, n * chans : (n + 1) * chans]
            if (half, o, p) in written:
                ybuf[half, o, p] += part
            else:
                ybuf[half, o, p] = part
                written.add((half, o, p))

    oring = [0]

    def finish(half, f):
        for slot in range(2):
            row = ROW_OF[half][slot]
            y0, y1, y2, y3 = [
                ybuf[half, f, p, slot * half_w : (slot + 1) * half_w]
                for p in range(POINTS)
            ]
            b = oring[0] % RING
            oring[0] += 1
            even = y0 + 0.5 * (y1 + y2)
            odd = 0.5 * (y1 - y2) - y3
            for c in range(chans // LANES):
                lanes = slice(c * LANES, (c + 1) * LANES)
                obuf[b, c, pl.ds(0, half_w, stride=2)] = even[:, lanes]
                obuf[b, c, pl.ds(1, half_w, stride=2)] = odd[:, lanes]
                total = obuf[b, c] + (
                    xbuf[f, row, :, lanes].astype(jnp.float32) + bias[:, lanes]
                )
                out_ref[f, row, :, lanes] = total.astype(jnp.bfloat16)

    rows = range(last + 1)
    x_copy(0).wait()
    for row in rows:
        own(0, row)
    for f in range(1, frames):
        x_copy(f).wait()
    for t, k in ((0, 0), (1, 0), (0, 2), (1, 2)):
        w_copy(t, k).wait()
    multiply(0, 0, 0)
    for row in rows:
        own(1, row)
    multiply(0, 0, 3)
    for t, k in ((2, 0), (2, 2), (0, 1), (1, 1), (2, 1)):
        w_copy(t, k).wait()
    multiply(0, 1, 0)
    own(2, 0)
    own(2, 1)
    multiply(0, 1, 3)
    own(2, 2)
    own(2, 3)
    multiply(0, 2, 0)
    add_weights(0, 0)
    multiply(0, 2, 3)
    add_weights(0, 1)
    multiply(0, 3, 0)
    for row in rows:
        own(3, row)
    multiply(0, 3, 3)
    add_weights(0, 2)
    multiply(0, 4, 0)
    add_weights(1, 0)
    multiply(0, 4, 3)
    multiply(0, 2, 1)
    add_weights(1, 1)
    multiply(0, 2, 2)
    multiply(0, 4, 1)
    add_weights(1, 2)
    multiply(0, 4, 2)
    multiply(0, 0, 1)
    add_weights(2, 0)
    multiply(0, 0, 2)
    finish(0, 0)
    finish(0, 1)
    add_weights(2, 1)
    add_weights(2, 2)
    multiply(0, 1, 1)
    multiply(0, 1, 2)

    def arrived(f):
        @pl.when(me > 0)
        def _():
            down(f).wait_recv()

        @pl.when(me < count - 1)
        def _():
            up(f).wait_recv()

    arrived(0)
    multiply(0, 3, 1)
    edge(0)
    multiply(0, 3, 2)
    arrived(1)
    for p in range(POINTS):
        multiply(1, 0, p)
        if p == 0:
            edge(1)
    finish(0, 2)
    finish(0, 3)
    for p in range(POINTS):
        multiply(1, 1, p)
    arrived(2)
    for p in range(POINTS):
        multiply(1, 2, p)
        if p == 0:
            edge(2)
    finish(1, 0)
    finish(1, 1)
    for p in range(POINTS):
        multiply(1, 3, p)
    arrived(3)
    edge(3)
    finish(1, 2)
    for p in range(POINTS):
        multiply(1, 4, p)
    finish(1, 3)

    @pl.when(me < count - 1)
    def _():
        for f in range(frames):
            down(f).wait_send()

    @pl.when(me > 0)
    def _():
        for f in range(frames):
            up(f).wait_send()


def hand_on(frames, held, to_ref, sem):
    copies = [
        pltpu.make_async_copy(held.at[f], to_ref.at[f], sem.at[f])
        for f in range(frames)
    ]
    for copy in copies:
        copy.start()
    for copy in copies:
        copy.wait()


def per_device(latents, gamma, weight, bias, intersection, ramp):
    frames, rows, width, chans = latents.shape
    count = lax.axis_size("rows")
    hbm = pl.BlockSpec(memory_space=pltpu.HBM)
    vmem = pl.BlockSpec(memory_space=pltpu.VMEM)
    made = pl.pallas_call(
        functools.partial(kernel, frames, width, chans, count),
        out_shape=pltpu.VMEM(latents.shape, latents.dtype),
        in_specs=[hbm, hbm, vmem, vmem, hbm, hbm],
        out_specs=vmem,
        scratch_shapes=[
            pltpu.VMEM((frames, rows, width, chans), jnp.bfloat16),
            pltpu.VMEM((frames, width, chans), jnp.bfloat16),
            pltpu.VMEM((frames, width, chans), jnp.bfloat16),
            pltpu.VMEM((TAPS, TAPS, TAPS, chans, chans), jnp.bfloat16),
            pltpu.VMEM((2, TAPS, TAPS, chans, chans), jnp.bfloat16),
            pltpu.VMEM((POINTS, frames, 8, width // 2, chans), jnp.bfloat16),
            pltpu.VMEM((RING, chans // LANES, width + 2 * PAD, LANES), jnp.float32),
            pltpu.VMEM((2, frames, POINTS, width, chans), jnp.float32),
            pltpu.VMEM((RING, chans // LANES, width, LANES), jnp.float32),
            pltpu.SMEM(intersection.shape, jnp.int32),
            pltpu.SMEM(ramp.shape, jnp.int32),
            pltpu.SemaphoreType.DMA((frames,)),
            pltpu.SemaphoreType.DMA((TAPS, TAPS)),
            pltpu.SemaphoreType.DMA((2,)),
            pltpu.SemaphoreType.DMA((2, frames)),
            pltpu.SemaphoreType.DMA((2, frames)),
        ],
        compiler_params=pltpu.CompilerParams(
            collective_id=0, has_side_effects=True, vmem_limit_bytes=56 * 1024 * 1024
        ),
    )(latents, weight, gamma, bias, intersection, ramp)
    return pl.pallas_call(
        functools.partial(hand_on, frames),
        out_shape=jax.ShapeDtypeStruct(latents.shape, latents.dtype),
        in_specs=[vmem],
        out_specs=hbm,
        scratch_shapes=[pltpu.SemaphoreType.DMA((frames,))],
        compiler_params=pltpu.CompilerParams(vmem_limit_bytes=16 * 1024 * 1024),
    )(made)


def solution(mesh):
    in_specs = (P("clips", "rows", None, None), P(), P(), P(), P("clips"), P("clips"))
    out_specs = P("clips", "rows", None, None)
    return jax.shard_map(
        per_device, mesh=mesh, in_specs=in_specs, out_specs=out_specs, check_vma=False
    )
```

time: 30.4 us -> 22.4 us (0.74)
  the two profiles are of different devices: /device:TPU:1 before, /device:TPU:25 now
where the time goes in v1:
time: 22.4 us; the launch traced here: 22.2 us
  Pallas kernels  22.1 us (99%)
    pallas_call x1, Pallas kernels, per_device(): pl.pallas_call(functools.partial(kernel, frames, width, chans, count), ou...  20.8 us
    pallas_call x1, Pallas kernels, per_device(): pl.pallas_call(functools.partial(hand_on, frames), out_shape=jax.ShapeDty...  1.3 us

profile of v1, /device:TPU:25, one launch (start us, length us, event | category | flops | bytes accessed | tf_op | source)
XLA Modules:
  0.0 22.2 jit_solution(6415862109486357167)
XLA Ops:
  0.0 20.8 %shard_map.64.held = bf16[4,4,160,384]{3,2,1,0:T(8,128)(2,1)S(1)} custom-call(bf16[4,4,160,384]{3,2,1,0:T(8,128)(2,1)} %x_ref.1, bf16[3,3,3,384,384]{4,3,2,1,0:T(8,128)(2,1)} %w_ref.1, f32[384]{0:T(512)} %gamma_ref.1, f32[384]{0:T(512)} %bias_ref.1, s32[16]{0:T(128)} %inter_hbm.1, s32[16]{0:T(128)} %ramp_hbm.1), custom_call_target="tpu_custom_call" | custom-call | tf_op jit(solution)/shard_map/pallas_call | solution.py:350
  20.8 1.3 %shard_map.65 = bf16[4,4,160,384]{3,2,1,0:T(8,128)(2,1)} custom-call(bf16[4,4,160,384]{3,2,1,0:T(8,128)(2,1)S(1)} %shard_map.64.held), custom_call_target="tpu_custom_call" | custom-call | tf_op jit(solution)/shard_map/pallas_call | solution.py:377

commit v2 on v1

--- a/solution.py
+++ b/solution.py
@@ -21,19 +21,23 @@
     ((ABOVE, ROW0, ROW1S), (ROW2, ROW3, BELOW)),
 )
 UNITS = (
-    ((0,), (0, 1), ((0, 1),)),
-    ((0,), (2,), ((2,),)),
-    ((1,), (1,), ((0,),)),
-    ((2, 1), (2, 3), ((0, 1), (1, 2))),
-    ((3,), (3,), ((0,),)),
+    ((1, 0), (1, 2), ((0, 1), (1, 2))),
+    ((2,), (2, 3), ((0, 1),)),
+    ((0,), (0,), ((0,),)),
+    ((1, 3), (3,), ((2,), (0,))),
 )
+A, B, C, D = range(4)
+STEP = 32
+DEEP = 64
+EARLY = ((0, 0), (0, 2), (1, 0), (1, 2))
+LATE = ((2, 0), (2, 2), (0, 1), (1, 1), (2, 1))
 
 
 def kernel(
     frames, width, chans, count,
-    x_ref, w_ref, gamma_ref, bias_ref, inter_hbm, ramp_hbm,
+    x_ref, w_ref, gamma_hbm, bias_hbm, inter_hbm, ramp_hbm,
     out_ref,
-    xbuf, top, bot, wbuf, gbuf, dbuf, act, ybuf, obuf, inter_ref, ramp_ref,
+    xbuf, top, bot, wbuf, gbuf, dbuf, act, ybuf, obuf, gamma_ref, bias_ref, inter_ref, ramp_ref,
     xsem, wsem, ssem, send_sem, recv_sem,
 ):
     me = lax.axis_index("rows")
@@ -63,6 +67,8 @@
     small = (
         pltpu.make_async_copy(inter_hbm, inter_ref, ssem.at[0]),
         pltpu.make_async_copy(ramp_hbm, ramp_ref, ssem.at[1]),
+        pltpu.make_async_copy(gamma_hbm, gamma_ref, ssem.at[2]),
+        pltpu.make_async_copy(bias_hbm, bias_ref, ssem.at[3]),
     )
     barrier = pltpu.get_barrier_semaphore()
 
@@ -82,7 +88,7 @@
         copy.start()
     for f in range(frames):
         x_copy(f).start()
-    for t, k in ((0, 0), (1, 0), (0, 2), (1, 2), (2, 0), (2, 2), (0, 1), (1, 1), (2, 1)):
+    for t, k in EARLY + LATE:
         w_copy(t, k).start()
 
     @pl.when(me == 0)
@@ -103,14 +109,14 @@
     peers = jnp.where(me > 0, 1, 0) + jnp.where(me < count - 1, 1, 0)
     pl.semaphore_wait(barrier, peers)
 
-    @pl.when(me < count - 1)
-    def _():
-        for f in range(frames):
+    for f in range(frames):
+
+        @pl.when(me < count - 1)
+        def _():
             down(f).start()
 
-    @pl.when(me > 0)
-    def _():
-        for f in range(frames):
+        @pl.when(me > 0)
+        def _():
             up(f).start()
 
     for copy in small:
@@ -132,29 +138,32 @@
     ring = [0]
 
     def activate(f, source, targets):
-        values = source.astype(jnp.float32)
-        square = jnp.mean(values * values, axis=-1, keepdims=True)
-        half = values * lax.rsqrt(square + 1e-06) * half_gamma
         b = ring[0] % RING
         ring[0] += 1
-        value = half + half * jnp.tanh(half)
+        for w0 in range(0, width, STEP):
+            values = source[w0 : w0 + STEP].astype(jnp.float32)
+            square = jnp.mean(values * values, axis=-1, keepdims=True)
+            half = values * lax.rsqrt(square + 1e-06) * half_gamma
+            value = half + half * jnp.tanh(half)
+            for c in range(chans // LANES):
+                lanes = slice(c * LANES, (c + 1) * LANES)
+                act[b, c, PAD + w0 : PAD + w0 + STEP] = value[:, lanes]
         for c in range(chans // LANES):
             lanes = slice(c * LANES, (c + 1) * LANES)
-            act[b, c, PAD : PAD + width] = value[:, lanes]
-            parts = [
-                act[b, c, pl.ds(PAD + at, half_w, stride=2)] for at in (-1, 0, 1, 2)
-            ]
             for version, scale in targets:
-                odd_b, even, odd, even_a = [
-                    (part if scale is None else part * scale[:, lanes]).astype(
-                        jnp.bfloat16
-                    )
-                    for part in parts
-                ]
-                dbuf[0, f, version, :, lanes] = odd_b - odd
-                dbuf[1, f, version, :, lanes] = even + odd
-                dbuf[2, f, version, :, lanes] = odd - even
-                dbuf[3, f, version, :, lanes] = even - even_a
+
+                def part(at):
+                    one = act[b, c, pl.ds(PAD + at, half_w, stride=2)]
+                    if scale is not None:
+                        one = one * scale[:, lanes]
+                    return one.astype(jnp.bfloat16)
+
+                odd = part(1)
+                dbuf[0, f, version, c] = part(-1) - odd
+                even = part(0)
+                dbuf[1, f, version, c] = even + odd
+                dbuf[2, f, version, c] = odd - even
+                dbuf[3, f, version, c] = even - part(2)
 
     own_targets = (
         ((ROW0, None),),
@@ -164,23 +173,34 @@
     )
 
     def own(f, row):
-        activate(f, xbuf[f, row], own_targets[row])
+        activate(f, xbuf.at[f, row], own_targets[row])
 
     def edge(f):
-        activate(f, top[f], ((ABOVE, a0),))
-        activate(f, bot[f], ((BELOW, live),))
+        activate(f, top.at[f], ((ABOVE, a0),))
+        activate(f, bot.at[f], ((BELOW, live),))
 
     def add_weights(t, h):
-        g0, g1, g2 = [wbuf[t, h, k].astype(jnp.float32) for k in range(TAPS)]
-        both = g0 + g2
-        gbuf[0, t, h] = (both + g1).astype(jnp.bfloat16)
-        gbuf[1, t, h] = (both - g1).astype(jnp.bfloat16)
+        for c in range(chans // LANES):
+            lanes = slice(c * LANES, (c + 1) * LANES)
+            for r0 in range(0, chans, DEEP):
+                at = slice(r0, r0 + DEEP)
+                first, middle, final = [
+                    wbuf[t, h, k, at, lanes].astype(jnp.float32) for k in range(TAPS)
+                ]
+                both = first + final
+                gbuf[0, t, h, c, at] = (both + middle).astype(jnp.bfloat16)
+                gbuf[1, t, h, c, at] = (both - middle).astype(jnp.bfloat16)
+
+    def across_lanes(ref):
+        return jnp.concatenate([ref[c] for c in range(chans // LANES)], axis=1)
 
     def filters(p, t):
         if p in (0, 3):
             k = 0 if p == 0 else TAPS - 1
             return jnp.concatenate([wbuf[t, h, k] for h in range(TAPS)], axis=0)
-        return jnp.concatenate([gbuf[p - 1, t, h] for h in range(TAPS)], axis=0)
+        return jnp.concatenate(
+            [across_lanes(gbuf.at[p - 1, t, h]) for h in range(TAPS)], axis=0
+        )
 
     written = set()
 
@@ -189,7 +209,12 @@
         left = jnp.concatenate(
             [
                 jnp.concatenate(
-                    [dbuf[p, f, version] for f in sources for version in reads], axis=1
+                    [
+                        across_lanes(dbuf.at[p, f, version])
+                        for f in sources
+                        for version in reads
+                    ],
+                    axis=1,
                 )
                 for reads in READS[half]
             ],
@@ -217,70 +242,24 @@
     def finish(half, f):
         for slot in range(2):
             row = ROW_OF[half][slot]
-            y0, y1, y2, y3 = [
-                ybuf[half, f, p, slot * half_w : (slot + 1) * half_w]
-                for p in range(POINTS)
-            ]
             b = oring[0] % RING
             oring[0] += 1
-            even = y0 + 0.5 * (y1 + y2)
-            odd = 0.5 * (y1 - y2) - y3
+            at = slice(slot * half_w, (slot + 1) * half_w)
             for c in range(chans // LANES):
                 lanes = slice(c * LANES, (c + 1) * LANES)
-                obuf[b, c, pl.ds(0, half_w, stride=2)] = even[:, lanes]
-                obuf[b, c, pl.ds(1, half_w, stride=2)] = odd[:, lanes]
+                y1, y2 = ybuf[half, f, 1, at, lanes], ybuf[half, f, 2, at, lanes]
+                obuf[b, c, pl.ds(0, half_w, stride=2)] = (
+                    ybuf[half, f, 0, at, lanes] + 0.5 * (y1 + y2)
+                )
+                obuf[b, c, pl.ds(1, half_w, stride=2)] = (
+                    0.5 * (y1 - y2) - ybuf[half, f, 3, at, lanes]
+                )
                 total = obuf[b, c] + (
                     xbuf[f, row, :, lanes].astype(jnp.float32) + bias[:, lanes]
                 )
                 out_ref[f, row, :, lanes] = total.astype(jnp.bfloat16)
 
     rows = range(last + 1)
-    x_copy(0).wait()
-    for row in rows:
-        own(0, row)
-    for f in range(1, frames):
-        x_copy(f).wait()
-    for t, k in ((0, 0), (1, 0), (0, 2), (1, 2)):
-        w_copy(t, k).wait()
-    multiply(0, 0, 0)
-    for row in rows:
-        own(1, row)
-    multiply(0, 0, 3)
-    for t, k in ((2, 0), (2, 2), (0, 1), (1, 1), (2, 1)):
-        w_copy(t, k).wait()
-    multiply(0, 1, 0)
-    own(2, 0)
-    own(2, 1)
-    multiply(0, 1, 3)
-    own(2, 2)
-    own(2, 3)
-    multiply(0, 2, 0)
-    add_weights(0, 0)
-    multiply(0, 2, 3)
-    add_weights(0, 1)
-    multiply(0, 3, 0)
-    for row in rows:
-        own(3, row)
-    multiply(0, 3, 3)
-    add_weights(0, 2)
-    multiply(0, 4, 0)
-    add_weights(1, 0)
-    multiply(0, 4, 3)
-    multiply(0, 2, 1)
-    add_weights(1, 1)
-    multiply(0, 2, 2)
-    multiply(0, 4, 1)
-    add_weights(1, 2)
-    multiply(0, 4, 2)
-    multiply(0, 0, 1)
-    add_weights(2, 0)
-    multiply(0, 0, 2)
-    finish(0, 0)
-    finish(0, 1)
-    add_weights(2, 1)
-    add_weights(2, 2)
-    multiply(0, 1, 1)
-    multiply(0, 1, 2)
 
     def arrived(f):
         @pl.when(me > 0)
@@ -291,33 +270,77 @@
         def _():
             up(f).wait_recv()
 
+    for f in range(2):
+        x_copy(f).wait()
+        for row in rows:
+            own(f, row)
+    for f in range(2, frames):
+        x_copy(f).wait()
+    for t, k in EARLY:
+        w_copy(t, k).wait()
+    multiply(0, C, 0)
+    own(2, 0)
+    own(2, 1)
+    multiply(0, C, 3)
+    own(2, 2)
+    own(2, 3)
+    multiply(0, B, 0)
+    multiply(0, B, 3)
+    for t, k in LATE:
+        w_copy(t, k).wait()
+    multiply(0, A, 0)
+    own(3, 0)
+    own(3, 1)
+    own(3, 2)
+    own(3, 3)
+    multiply(0, A, 3)
+    for h in range(TAPS):
+        add_weights(0, h)
+    multiply(0, D, 0)
+    add_weights(1, 0)
+    multiply(0, D, 3)
+    add_weights(1, 1)
+    multiply(0, C, 1)
+    add_weights(1, 2)
+    multiply(0, C, 2)
+    add_weights(2, 0)
+    multiply(0, B, 1)
+    add_weights(2, 1)
+    multiply(0, B, 2)
+    add_weights(2, 2)
+    finish(0, 0)
+    multiply(0, A, 1)
+    multiply(0, A, 2)
+    finish(0, 1)
     arrived(0)
-    multiply(0, 3, 1)
+    arrived(1)
+    multiply(0, D, 1)
     edge(0)
-    multiply(0, 3, 2)
-    arrived(1)
+    multiply(0, D, 2)
     for p in range(POINTS):
-        multiply(1, 0, p)
-        if p == 0:
-            edge(1)
+        multiply(1, C, p)
+    edge(1)
     finish(0, 2)
+    multiply(1, A, 0)
     finish(0, 3)
-    for p in range(POINTS):
-        multiply(1, 1, p)
+    multiply(1, A, 1)
+    finish(1, 0)
+    multiply(1, A, 2)
     arrived(2)
-    for p in range(POINTS):
-        multiply(1, 2, p)
-        if p == 0:
-            edge(2)
-    finish(1, 0)
+    arrived(3)
+    multiply(1, A, 3)
+    edge(2)
+    edge(3)
+    multiply(1, B, 0)
+    multiply(1, B, 1)
     finish(1, 1)
-    for p in range(POINTS):
-        multiply(1, 3, p)
-    arrived(3)
-    edge(3)
+    multiply(1, B, 2)
+    multiply(1, B, 3)
+    multiply(1, D, 0)
     finish(1, 2)
-    for p in range(POINTS):
-        multiply(1, 4, p)
+    multiply(1, D, 1)
+    multiply(1, D, 2)
+    multiply(1, D, 3)
     finish(1, 3)
 
     @pl.when(me < count - 1)
@@ -350,23 +373,27 @@
     made = pl.pallas_call(
         functools.partial(kernel, frames, width, chans, count),
         out_shape=pltpu.VMEM(latents.shape, latents.dtype),
-        in_specs=[hbm, hbm, vmem, vmem, hbm, hbm],
+        in_specs=[hbm] * 6,
         out_specs=vmem,
         scratch_shapes=[
             pltpu.VMEM((frames, rows, width, chans), jnp.bfloat16),
             pltpu.VMEM((frames, width, chans), jnp.bfloat16),
             pltpu.VMEM((frames, width, chans), jnp.bfloat16),
             pltpu.VMEM((TAPS, TAPS, TAPS, chans, chans), jnp.bfloat16),
-            pltpu.VMEM((2, TAPS, TAPS, chans, chans), jnp.bfloat16),
-            pltpu.VMEM((POINTS, frames, 8, width // 2, chans), jnp.bfloat16),
+            pltpu.VMEM((2, TAPS, TAPS, chans // LANES, chans, LANES), jnp.bfloat16),
+            pltpu.VMEM(
+                (POINTS, frames, 8, chans // LANES, width // 2, LANES), jnp.bfloat16
+            ),
             pltpu.VMEM((RING, chans // LANES, width + 2 * PAD, LANES), jnp.float32),
             pltpu.VMEM((2, frames, POINTS, width, chans), jnp.float32),
             pltpu.VMEM((RING, chans // LANES, width, LANES), jnp.float32),
+            pltpu.VMEM(gamma.shape, jnp.float32),
+            pltpu.VMEM(bias.shape, jnp.float32),
             pltpu.SMEM(intersection.shape, jnp.int32),
             pltpu.SMEM(ramp.shape, jnp.int32),
             pltpu.SemaphoreType.DMA((frames,)),
             pltpu.SemaphoreType.DMA((TAPS, TAPS)),
-            pltpu.SemaphoreType.DMA((2,)),
+            pltpu.SemaphoreType.DMA((4,)),
             pltpu.SemaphoreType.DMA((2, frames)),
             pltpu.SemaphoreType.DMA((2, frames)),
         ],

time: 22.4 us -> 21.5 us (0.960)
  Pallas kernels: 22.1 us -> 21.2 us
    pallas_call x1, Pallas kernels: 20.8 us -> 19.9 us  [per_device(): pl.pallas_call(functools.partial(kernel, frames, width, chans, count), ou...]
where the time goes in v2:
time: 21.5 us; the launch traced here: 21.4 us
  Pallas kernels  21.2 us (99%)
    pallas_call x1, Pallas kernels, per_device(): pl.pallas_call(functools.partial(kernel, frames, width, chans, count), ou...  19.9 us
    pallas_call x1, Pallas kernels, per_device(): pl.pallas_call(functools.partial(hand_on, frames), out_shape=jax.ShapeDty...  1.3 us

profile of v2, /device:TPU:25, one launch (start us, length us, event | category | flops | bytes accessed | tf_op | source)
XLA Modules:
  0.0 21.4 jit_solution(6373083213563454155)
XLA Ops:
  0.0 19.9 %shard_map.64.held = bf16[4,4,160,384]{3,2,1,0:T(8,128)(2,1)S(1)} custom-call(bf16[4,4,160,384]{3,2,1,0:T(8,128)(2,1)} %x_ref.1, bf16[3,3,3,384,384]{4,3,2,1,0:T(8,128)(2,1)} %w_ref.1, f32[384]{0:T(512)} %gamma_hbm.1, f32[384]{0:T(512)} %bias_hbm.1, s32[16]{0:T(128)} %inter_hbm.1, s32[16]{0:T(128)} %ramp_hbm.1), custom_call_target="tpu_custom_call" | custom-call | tf_op jit(solution)/shard_map/pallas_call | solution.py:373
  19.9 1.3 %shard_map.65 = bf16[4,4,160,384]{3,2,1,0:T(8,128)(2,1)} custom-call(bf16[4,4,160,384]{3,2,1,0:T(8,128)(2,1)S(1)} %shard_map.64.held), custom_call_target="tpu_custom_call" | custom-call | tf_op jit(solution)/shard_map/pallas_call | solution.py:404

commit v3 on v2

--- a/solution.py
+++ b/solution.py
@@ -29,8 +29,12 @@
 A, B, C, D = range(4)
 STEP = 32
 DEEP = 64
-EARLY = ((0, 0), (0, 2), (1, 0), (1, 2))
-LATE = ((2, 0), (2, 2), (0, 1), (1, 1), (2, 1))
+XPARTS = (pl.ds(0, 1), pl.ds(1, 1), pl.ds(2, 2))
+WPARTS = (
+    (pl.ds(1, 2), 0), (pl.ds(1, 2), 2), (pl.ds(0, 1), 0), (pl.ds(0, 1), 2),
+    (pl.ds(0, TAPS), 1),
+)
+PAIR = 2
 
 
 def kernel(
@@ -44,24 +48,28 @@
     last = xbuf.shape[1] - 1
     half_w = width // 2
 
-    def x_copy(f):
-        return pltpu.make_async_copy(x_ref.at[f], xbuf.at[f], xsem.at[f])
-
-    def w_copy(t, k):
-        return pltpu.make_async_copy(
-            w_ref.at[TAPS - 1 - t, :, k], wbuf.at[t, :, k], wsem.at[t, k]
-        )
-
-    def down(f):
+    def x_copy(n):
+        at = XPARTS[n]
+        return pltpu.make_async_copy(x_ref.at[at], xbuf.at[at], xsem.at[n])
+
+    def w_copy(n):
+        t, k = WPARTS[n]
+        return pltpu.make_async_copy(w_ref.at[t, :, k], wbuf.at[t, :, k], wsem.at[n])
+
+    def down(n):
+        at = pl.ds(n * PAIR, PAIR)
         return pltpu.make_async_remote_copy(
-            src_ref=x_ref.at[f, last], dst_ref=top.at[f], send_sem=send_sem.at[0, f],
-            recv_sem=recv_sem.at[0, f], device_id={"rows": me + 1}, device_id_type=MESH,
-        )
-
-    def up(f):
+            src_ref=x_ref.at[at, last], dst_ref=top.at[at],
+            send_sem=send_sem.at[0, n], recv_sem=recv_sem.at[0, n],
+            device_id={"rows": me + 1}, device_id_type=MESH,
+        )
+
+    def up(n):
+        at = pl.ds(n * PAIR, PAIR)
         return pltpu.make_async_remote_copy(
-            src_ref=x_ref.at[f, 0], dst_ref=bot.at[f], send_sem=send_sem.at[1, f],
-            recv_sem=recv_sem.at[1, f], device_id={"rows": me - 1}, device_id_type=MESH,
+            src_ref=x_ref.at[at, 0], dst_ref=bot.at[at],
+            send_sem=send_sem.at[1, n], recv_sem=recv_sem.at[1, n],
+            device_id={"rows": me - 1}, device_id_type=MESH,
         )
 
     small = (
@@ -86,10 +94,10 @@
 
     for copy in small:
         copy.start()
-    for f in range(frames):
-        x_copy(f).start()
-    for t, k in EARLY + LATE:
-        w_copy(t, k).start()
+    for n in range(len(XPARTS)):
+        x_copy(n).start()
+    for n in range(len(WPARTS)):
+        w_copy(n).start()
 
     @pl.when(me == 0)
     def _():
@@ -109,15 +117,15 @@
     peers = jnp.where(me > 0, 1, 0) + jnp.where(me < count - 1, 1, 0)
     pl.semaphore_wait(barrier, peers)
 
-    for f in range(frames):
+    for n in range(frames // PAIR):
 
         @pl.when(me < count - 1)
         def _():
-            down(f).start()
+            down(n).start()
 
         @pl.when(me > 0)
         def _():
-            up(f).start()
+            up(n).start()
 
     for copy in small:
         copy.wait()
@@ -185,7 +193,7 @@
             for r0 in range(0, chans, DEEP):
                 at = slice(r0, r0 + DEEP)
                 first, middle, final = [
-                    wbuf[t, h, k, at, lanes].astype(jnp.float32) for k in range(TAPS)
+                    wbuf[TAPS - 1 - t, h, k, at, lanes].astype(jnp.float32) for k in range(TAPS)
                 ]
                 both = first + final
                 gbuf[0, t, h, c, at] = (both + middle).astype(jnp.bfloat16)
@@ -197,7 +205,7 @@
     def filters(p, t):
         if p in (0, 3):
             k = 0 if p == 0 else TAPS - 1
-            return jnp.concatenate([wbuf[t, h, k] for h in range(TAPS)], axis=0)
+            return jnp.concatenate([wbuf[TAPS - 1 - t, h, k] for h in range(TAPS)], axis=0)
         return jnp.concatenate(
             [across_lanes(gbuf.at[p - 1, t, h]) for h in range(TAPS)], axis=0
         )
@@ -274,10 +282,9 @@
         x_copy(f).wait()
         for row in rows:
             own(f, row)
-    for f in range(2, frames):
-        x_copy(f).wait()
-    for t, k in EARLY:
-        w_copy(t, k).wait()
+    x_copy(2).wait()
+    w_copy(0).wait()
+    w_copy(1).wait()
     multiply(0, C, 0)
     own(2, 0)
     own(2, 1)
@@ -286,8 +293,8 @@
     own(2, 3)
     multiply(0, B, 0)
     multiply(0, B, 3)
-    for t, k in LATE:
-        w_copy(t, k).wait()
+    for n in range(2, len(WPARTS)):
+        w_copy(n).wait()
     multiply(0, A, 0)
     own(3, 0)
     own(3, 1)
@@ -313,7 +320,6 @@
     multiply(0, A, 2)
     finish(0, 1)
     arrived(0)
-    arrived(1)
     multiply(0, D, 1)
     edge(0)
     multiply(0, D, 2)
@@ -326,12 +332,11 @@
     multiply(1, A, 1)
     finish(1, 0)
     multiply(1, A, 2)
-    arrived(2)
-    arrived(3)
     multiply(1, A, 3)
+    arrived(1)
     edge(2)
+    multiply(1, B, 0)
     edge(3)
-    multiply(1, B, 0)
     multiply(1, B, 1)
     finish(1, 1)
     multiply(1, B, 2)
@@ -345,13 +350,13 @@
 
     @pl.when(me < count - 1)
     def _():
-        for f in range(frames):
-            down(f).wait_send()
+        for n in range(frames // PAIR):
+            down(n).wait_send()
 
     @pl.when(me > 0)
     def _():
-        for f in range(frames):
-            up(f).wait_send()
+        for n in range(frames // PAIR):
+            up(n).wait_send()
 
 
 def hand_on(frames, held, to_ref, sem):
@@ -391,11 +396,11 @@
             pltpu.VMEM(bias.shape, jnp.float32),
             pltpu.SMEM(intersection.shape, jnp.int32),
             pltpu.SMEM(ramp.shape, jnp.int32),
-            pltpu.SemaphoreType.DMA((frames,)),
-            pltpu.SemaphoreType.DMA((TAPS, TAPS)),
+            pltpu.SemaphoreType.DMA((len(XPARTS),)),
+            pltpu.SemaphoreType.DMA((len(WPARTS),)),
             pltpu.SemaphoreType.DMA((4,)),
-            pltpu.SemaphoreType.DMA((2, frames)),
-            pltpu.SemaphoreType.DMA((2, frames)),
+            pltpu.SemaphoreType.DMA((2, frames // PAIR)),
+            pltpu.SemaphoreType.DMA((2, frames // PAIR)),
         ],
         compiler_params=pltpu.CompilerParams(
             collective_id=0, has_side_effects=True, vmem_limit_bytes=56 * 1024 * 1024

time: 21.5 us -> 21.1 us (0.981)
  Pallas kernels: 21.2 us -> 20.8 us
    pallas_call x1, Pallas kernels: 19.9 us -> 19.5 us  [per_device(): pl.pallas_call(functools.partial(kernel, frames, width, chans, count), ou...]
where the time goes in v3:
time: 21.1 us; the launch traced here: 21 us
  Pallas kernels  20.8 us (99%)
    pallas_call x1, Pallas kernels, per_device(): pl.pallas_call(functools.partial(kernel, frames, width, chans, count), ou...  19.5 us
    pallas_call x1, Pallas kernels, per_device(): pl.pallas_call(functools.partial(hand_on, frames), out_shape=jax.ShapeDty...  1.3 us

profile of v3, /device:TPU:25, one launch (start us, length us, event | category | flops | bytes accessed | tf_op | source)
XLA Modules:
  0.0 21.0 jit_solution(1169187075540705576)
XLA Ops:
  0.0 19.5 %shard_map.64.held = bf16[4,4,160,384]{3,2,1,0:T(8,128)(2,1)S(1)} custom-call(bf16[4,4,160,384]{3,2,1,0:T(8,128)(2,1)} %x_ref.1, bf16[3,3,3,384,384]{4,3,2,1,0:T(8,128)(2,1)} %w_ref.1, f32[384]{0:T(512)} %gamma_hbm.1, f32[384]{0:T(512)} %bias_hbm.1, s32[16]{0:T(128)} %inter_hbm.1, s32[16]{0:T(128)} %ramp_hbm.1), custom_call_target="tpu_custom_call" | custom-call | tf_op jit(solution)/shard_map/pallas_call | solution.py:378
  19.5 1.3 %shard_map.65 = bf16[4,4,160,384]{3,2,1,0:T(8,128)(2,1)} custom-call(bf16[4,4,160,384]{3,2,1,0:T(8,128)(2,1)S(1)} %shard_map.64.held), custom_call_target="tpu_custom_call" | custom-call | tf_op jit(solution)/shard_map/pallas_call | solution.py:409

commit v4 on v3

--- a/solution.py
+++ b/solution.py
@@ -283,21 +283,21 @@
         for row in rows:
             own(f, row)
     x_copy(2).wait()
+    own(2, 0)
+    own(2, 1)
     w_copy(0).wait()
     w_copy(1).wait()
     multiply(0, C, 0)
-    own(2, 0)
-    own(2, 1)
-    multiply(0, C, 3)
     own(2, 2)
     own(2, 3)
+    multiply(0, C, 3)
+    own(3, 0)
     multiply(0, B, 0)
+    own(3, 1)
     multiply(0, B, 3)
     for n in range(2, len(WPARTS)):
         w_copy(n).wait()
     multiply(0, A, 0)
-    own(3, 0)
-    own(3, 1)
     own(3, 2)
     own(3, 3)
     multiply(0, A, 3)

time: 21.1 us -> 21.1 us (level)
  no operation moved by 1% of the time
where the time goes in v4:
time: 21.1 us; the launch traced here: 21 us
  Pallas kernels  20.8 us (99%)
    pallas_call x1, Pallas kernels, per_device(): pl.pallas_call(functools.partial(kernel, frames, width, chans, count), ou...  19.5 us
    pallas_call x1, Pallas kernels, per_device(): pl.pallas_call(functools.partial(hand_on, frames), out_shape=jax.ShapeDty...  1.3 us

profile of v4, /device:TPU:25, one launch (start us, length us, event | category | flops | bytes accessed | tf_op | source)
XLA Modules:
  0.0 21.0 jit_solution(10815051496135141538)
XLA Ops:
  0.0 19.5 %shard_map.64.held = bf16[4,4,160,384]{3,2,1,0:T(8,128)(2,1)S(1)} custom-call(bf16[4,4,160,384]{3,2,1,0:T(8,128)(2,1)} %x_ref.1, bf16[3,3,3,384,384]{4,3,2,1,0:T(8,128)(2,1)} %w_ref.1, f32[384]{0:T(512)} %gamma_hbm.1, f32[384]{0:T(512)} %bias_hbm.1, s32[16]{0:T(128)} %inter_hbm.1, s32[16]{0:T(128)} %ramp_hbm.1), custom_call_target="tpu_custom_call" | custom-call | tf_op jit(solution)/shard_map/pallas_call | solution.py:378
  19.5 1.3 %shard_map.65 = bf16[4,4,160,384]{3,2,1,0:T(8,128)(2,1)} custom-call(bf16[4,4,160,384]{3,2,1,0:T(8,128)(2,1)S(1)} %shard_map.64.held), custom_call_target="tpu_custom_call" | custom-call | tf_op jit(solution)/shard_map/pallas_call | solution.py:409
